TPU v7x, 32 devices: a whole 2x2x4 slice. The times are simulated.
32 devices in a mesh: grp: 2 (over x), ma: 16 (over z, y, core).
Axes of the slice: x: 2, y: 2, z: 4, core: 2. Of those that a mesh axis runs over, the one named last changes fastest.
Arguments:
- vis: float32 [16384, 2, 256], P(('grp', 'ma')), parts along dimension 0, may hold values from -6 to 6
- transfer: bfloat16 [32, 2, 256, 1024], P(('grp', 'ma')), parts along dimension 0, may hold values from -0.1875 to 0.1875
- band_start: int32 [2], P('grp'), parts along dimension 0, may hold values from 0 to 8176
- comp_index: int32 [2048], P(('grp', 'ma')), parts along dimension 0, may hold values from 0 to 16383
- comp_amp: int32 [2048, 2], P(('grp', 'ma')), parts along dimension 0, may hold values from -4096 to 4096
Outputs:
- residual_alm: float32 [32, 2, 1024], P(('grp', 'ma')), parts along dimension 0
There are 2 independent parts, one for each index of `grp`. A program takes and returns all parts, laid end to end along the dimension named above; each array names one. Nothing has to cross between parts.
All inputs are finite; a program needn't handle non-finite values.
Results may differ from a plain program's by a relative error of at most 0.003.
Values sent between devices are 32-bit elements; how exact they have to be, the bound alone decides.
A program may use at most 64 MiB of HBM per device.

v0:
```python
import math

import jax
import jax.numpy as jnp
from jax import lax
from jax.sharding import PartitionSpec as P

SIDEREAL_TICKS = 8192


def trig_pair_lookup(azimuthal_orders, tick_moments):
    rotation_radians = azimuthal_orders[:, None] * tick_moments[None, :] % SIDEREAL_TICKS
    angle = rotation_radians.astype(jnp.float32) * (2.0 * math.pi / SIDEREAL_TICKS)
    return jnp.concatenate([jnp.cos(angle), jnp.sin(angle)], 0)


def combine_parts(product, row_count):
    product = product.reshape(2, row_count, 2, -1)
    scale = 1.0 / math.sqrt(SIDEREAL_TICKS)
    real_part = (product[0, :, 0] + product[1, :, 1]) * scale
    imag_part = (product[0, :, 1] - product[1, :, 0]) * scale
    return jnp.stack([real_part, imag_part], 1)


def body(vis, transfer, band_start, comp_index, comp_amp):
    ma_count = lax.axis_size("ma")
    device_rank = lax.axis_index("ma")
    m_local = transfer.shape[0]
    width = transfer.shape[3]
    modes = m_local * ma_count
    regrouped = lax.all_to_all(vis, "ma", split_axis=2, concat_axis=0, tiled=True)
    azimuthal_orders = band_start[0] + jnp.arange(modes, dtype=jnp.int32)
    trig_pair = trig_pair_lookup(azimuthal_orders, jnp.arange(SIDEREAL_TICKS, dtype=jnp.int32))
    flat_visibility = regrouped.reshape(SIDEREAL_TICKS, -1)
    product = jnp.dot(
        trig_pair,
        flat_visibility,
        precision=lax.Precision.HIGHEST,
        preferred_element_type=jnp.float32,
    )
    local_spectra = combine_parts(product, modes)
    spectra = lax.all_to_all(local_spectra, "ma", split_axis=0, concat_axis=2, tiled=True)
    index_all, amp_all = (
        lax.all_gather(comp_index, "ma", axis=0, tiled=True),
        lax.all_gather(comp_amp, "ma", axis=0, tiled=True),
    )
    slots = m_local * width
    offset = index_all - device_rank * slots
    inside = (offset >= 0) & (offset < slots)
    target = jnp.where(inside, offset, slots)
    summed = jax.ops.segment_sum(amp_all, target, num_segments=slots + 1)[:slots]
    model_alm = (
        (summed.astype(jnp.float32) * (1.0 / 1024.0))
        .astype(jnp.bfloat16)
        .reshape(m_local, width, 2)
    )
    predicted = jnp.einsum(
        "mcbl,mlk->mcbk", transfer, model_alm, preferred_element_type=jnp.float32
    )
    pred_real = predicted[:, 0, :, 0] - predicted[:, 1, :, 1]
    pred_imag = predicted[:, 0, :, 1] + predicted[:, 1, :, 0]
    resid_vis = (spectra - jnp.stack([pred_real, pred_imag], 1)).astype(jnp.bfloat16)
    projected = jnp.einsum(
        "mcbl,mkb->mkcl", transfer, resid_vis, preferred_element_type=jnp.float32
    )
    alm_real = projected[:, 0, 0] + projected[:, 1, 1]
    alm_imag = projected[:, 1, 0] - projected[:, 0, 1]
    return jnp.stack([alm_real, alm_imag], 1)


def solution(mesh):
    in_specs = (
        P(("grp", "ma"), None, None),
        P(("grp", "ma"), None, None, None),
        P("grp"),
        P(("grp", "ma")),
        P(("grp", "ma"), None),
    )
    out_specs = P(("grp", "ma"), None, None)
    return jax.shard_map(body, mesh=mesh, in_specs=in_specs, out_specs=out_specs, check_vma=False)
```

profile of v0, /device:TPU:0, one launch (start us, length us, event | category | flops | bytes accessed | tf_op | source)
XLA Modules:
  0.0 85.7 jit_solution(13697554280180083877)
XLA Ops:
  0.0 3.7 %copy.34 = f32[512,2,256]{0,1,2:T(2,128)} copy(f32[512,2,256]{2,1,0:T(2,128)} %param.5) | data formatting | bytes 2097152 | tf_op args[0]
  3.7 7.4 %all-to-all-start = ((f32[512,2,256]{0,1,2:T(2,128)}), f32[512,2,256]{0,1,2:T(2,128)S(1)}, u32[]{:S(2)}, u32[]{:S(2)}) async-start(f32[512,2,256]{0,1,2:T(2,128)} %copy.34), calls=%async_computation | async-start | bytes 2097152 | tf_op jit(solution)/shard_map/all_to_all | solution.py:31
  11.8 0.6 copy-done.3
  12.4 0.6 dynamic-slice
  13.7 0.6 copy-done.2
  14.3 0.2 dynamic-update-slice
  14.5 23.3 %all-reduce = s32[1024]{0:T(1024)S(1)} all-reduce(s32[1024]{0:T(1024)S(1)} %dynamic-update-slice), channel_id=1, replica_groups=mesh['grp'=2,'ma'=16] {'ma'}, use_global_device_ids=true, to_apply=%add | all-reduce | flops 1024 | bytes 8192
  37.8 0.7 copy-done.1
  38.5 19.4 %all-gather = s32[16,64,2]{1,2,0:T(2,128)S(1)} all-gather(s32[1,64,2]{1,2,0:T(2,128)S(1)} %bitcast.60), channel_id=1, replica_groups=mesh['grp'=2,'ma'=16] {'ma'}, dimensions={0}, use_global_device_ids=true | all-gather | bytes 8704 | tf_op jit(solution)/shard_map/all_gather | solution.py:45
  58.0 0.2 copy.43
  58.2 7.3 %scatter_custom_fusion = s32[1025,2]{1,0:T(8,128)S(1)} fusion(s32[1024]{0:T(1024)S(1)} %and_select_fusion, s32[1024,2]{1,0:T(8,128)S(1)} %bitcast.59, s32[]{:T(128)} %constant.9.clone.1), kind=kCustom, calls=%fused_computation.16 | custom fusion | flops 2048 | bytes 8204 | tf_op jit(solution)/shard_map/scatter-add | solution.py:51
  65.6 0.1 copy.47
  65.7 0.4 convolution_bitcast_fusion.1
  66.1 2.1 %fusion.11 = (f32[16,8192]{1,0:T(8,128)S(1)}, f32[16,8192]{1,0:T(8,128)S(1)}) fusion(s32[16]{0:T(128)S(1)} %iota_add_fusion), kind=kLoop, calls=%fused_computation.19 | loop fusion | flops 1835008 | bytes 1048640 | tf_op jit(solution)/shard_map/cos | solution.py:14
  68.3 0.2 copy.35
  68.5 0.6 copy.36
  69.1 0.6 copy.46
  69.7 4.4 %fusion.22 = f32[2,16,2,16]{3,1,2,0:T(8,128)S(1)} fusion(f32[2,16,8192,1]{2,1,3,0:T(8,128)S(1)} %bitcast.55, f32[2,16,8192,1]{2,1,0,3:T(8,128)S(1)} %bitcast.56), kind=kOutput, calls=%fused_computation.41 | convolution fusion | flops 100663296 | bytes 2101248 | tf_op jit(solution)/shard_map/dot_general | solution.py:35
  74.2 0.6 copy.37
  74.8 3.5 %all-to-all-start.1 = ((f32[16,2,16]{2,1,0:T(2,128)}), f32[16,2,16]{2,1,0:T(2,128)S(1)}, u32[]{:S(2)}, u32[]{:S(2)}) async-start(f32[16,2,16]{2,1,0:T(2,128)} %copy.37), calls=%async_computation.1 | async-start | bytes 32768 | tf_op jit(solution)/shard_map/all_to_all | solution.py:42
  78.5 6.3 %all-to-all-done.1 = f32[16,2,16]{2,1,0:T(2,128)S(1)} async-done(((f32[16,2,16]{2,1,0:T(2,128)}), f32[16,2,16]{2,1,0:T(2,128)S(1)}, u32[]{:S(2)}, u32[]{:S(2)}) %all-to-all-start.1) | async-done | bytes 2080 | tf_op jit(solution)/shard_map/all_to_all | solution.py:42
  84.8 0.1 reshape.206
  84.8 0.2 convolution_bitcast_fusion
  85.1 0.6 pad_maximum_fusion.2
  (18 shorter events, 0.4 us)
Async XLA Ops:
  0.0 65.7 %copy-start = (bf16[1,2,256,1024]{3,2,1,0:T(8,128)(2,1)S(1)}, bf16[1,2,256,1024]{3,2,1,0:T(8,128)(2,1)}, u32[]{:S(2)}) copy-start(bf16[1,2,256,1024]{3,2,1,0:T(8,128)(2,1)} %param.6) | copy-start | bytes 3145732
  3.7 64.6 %all-to-all-start = ((f32[512,2,256]{0,1,2:T(2,128)}), f32[512,2,256]{0,1,2:T(2,128)S(1)}, u32[]{:S(2)}, u32[]{:S(2)}) async-start(f32[512,2,256]{0,1,2:T(2,128)} %copy.34), calls=%async_computation | async-start | bytes 2097152 | tf_op jit(solution)/shard_map/all_to_all | solution.py:31
  11.8 0.7 copy-start.3
  13.7 0.7 copy-start.2
  37.8 0.7 copy-start.1
  74.8 9.9 %all-to-all-start.1 = ((f32[16,2,16]{2,1,0:T(2,128)}), f32[16,2,16]{2,1,0:T(2,128)S(1)}, u32[]{:S(2)}, u32[]{:S(2)}) async-start(f32[16,2,16]{2,1,0:T(2,128)} %copy.37), calls=%async_computation.1 | async-start | bytes 32768 | tf_op jit(solution)/shard_map/all_to_all | solution.py:42
where the time goes:
time: 86.1 us; the launch traced here: 85.7 us
  blocking collectives  42.8 us (50%)
  starting transfers between devices  10.9 us (13%)
  other arithmetic  10.2 us (12%)
  local copies, waits for them, and re-layouts  9.1 us (11%)
  waiting for transfers between devices  6.28 us (7%)
  matrix products  5.05 us (6%)
  between operations  1.48 us (2%)
    unnamed x1, blocking collectives  23.3 us
    all_gather x1, blocking collectives, body(): lax.all_gather(comp_amp, 'ma', axis=0, tiled=True)  19.4 us
    unnamed x15, local copies, waits for them, and re-layouts  7.42 us
    all_to_all x1, starting transfers between devices, body(): lax.all_to_all(vis, 'ma', split_axis=2, concat_axis=0, tiled=True)  7.39 us
    scatter-add x1, other arithmetic, body(): jax.ops.segment_sum(amp_all, target, num_segments=slots + 1)[:slots]  7.26 us
    all_to_all x1, waiting for transfers between devices, body(): lax.all_to_all(local_spectra, 'ma', split_axis=0, concat_axis=2, tiled=True)  6.28 us
    dot_general x1, matrix products, body(): jnp.dot(trig_pair, flat_visibility, precision=lax.Precision.HIGHEST, pref...  4.42 us
    all_to_all x1, starting transfers between devices, body(): lax.all_to_all(local_spectra, 'ma', split_axis=0, concat_axis=2, tiled=True)  3.47 us
  transfers between devices with their start and end apart: 2, of which 1 were waited for; matrix products, arithmetic and copies ran while one was open for 13% of the time, Pallas kernels for 0%

commit v1 on v0

v1 whole, which is shorter than its diff:
```python
import functools
import math

import jax
import jax.numpy as jnp
from jax import lax
from jax.experimental import pallas as pl
from jax.experimental.pallas import tpu as pltpu
from jax.sharding import PartitionSpec as P

LANES = 128
F32 = jnp.float32
BF16 = jnp.bfloat16
MESH = pl.DeviceIdType.MESH


def trig_pair(order_start, tick_start, modes, ticks, period):
    order = order_start + lax.broadcasted_iota(jnp.int32, (modes, ticks), 0)
    tick = tick_start + lax.broadcasted_iota(jnp.int32, (modes, ticks), 1)
    phase = (order * tick) & (period - 1)
    quarter = period // 4
    shift = quarter.bit_length() - 1
    quadrant = (phase + quarter // 2) >> shift
    x = (phase - (quadrant << shift)).astype(F32) * (2.0 * math.pi / period)
    z = x * x
    sin_x = x * (1.0 + z * (-1.0 / 6 + z * (1.0 / 120 + z * (-1.0 / 5040 + z * (1.0 / 362880)))))
    cos_x = 1.0 + z * (-0.5 + z * (1.0 / 24 + z * (-1.0 / 720 + z * (1.0 / 40320))))
    swap = (quadrant & 1) == 1
    cos = jnp.where(swap, sin_x, cos_x)
    sin = jnp.where(swap, cos_x, sin_x)
    cos = jnp.where(((quadrant + 1) & 2) == 2, -cos, cos)
    sin = jnp.where((quadrant & 2) == 2, -sin, sin)
    return cos, sin


def split(values):
    high = values.astype(BF16)
    return high, (values - high.astype(F32)).astype(BF16)


def mul(a, b, contract=((1,), (0,))):
    return lax.dot_general(a, b, (contract, ((), ())), preferred_element_type=F32)


def kernel(
    n, ticks, tiles, count, width,
    vis_hbm, transfer_hbm, start_ref, index_ref, amp_ref, out_ref,
    vis, transfer, comp_out, comp_in, spec_out, spec_in,
    vis_sem, transfer_sem, comp_send, comp_recv, spec_send, spec_recv,
):
    me = lax.axis_index("ma")
    vis_copy = pltpu.make_async_copy(vis_hbm, vis, vis_sem)
    transfer_copy = pltpu.make_async_copy(transfer_hbm, transfer, transfer_sem)
    vis_copy.start()
    transfer_copy.start()

    def peers(step):
        if n <= 32:
            for offset in range(1, n):
                step(offset)
        else:
            pl.loop(1, n)(step)

    def peer(offset):
        target = me + offset
        return jnp.where(target >= n, target - n, target)

    barrier = pltpu.get_barrier_semaphore()

    def greet(offset):
        pl.semaphore_signal(barrier, inc=1, device_id={"ma": peer(offset)}, device_id_type=MESH)

    peers(greet)

    comp_out[...] = jnp.full(comp_out.shape, -1, jnp.int32)
    comp_out[0:1, 0:count] = index_ref[...]
    comp_out[1:3, 0:count] = amp_ref[...]
    comp_in[n - 1] = comp_out[...]
    pl.semaphore_wait(barrier, n - 1)

    def send_comp(offset):
        pltpu.make_async_remote_copy(
            src_ref=comp_out, dst_ref=comp_in.at[offset - 1],
            send_sem=comp_send, recv_sem=comp_recv,
            device_id={"ma": peer(offset)}, device_id_type=MESH,
        ).start()

    peers(send_comp)

    cos, sin = trig_pair(start_ref[0], me * ticks, n, ticks, ticks * n)
    (cos_high, cos_low), (sin_high, sin_low) = split(cos), split(sin)
    high_rows = jnp.concatenate([cos_high, sin_high], 0)
    all_rows = jnp.concatenate([cos_high, sin_high, cos_low, sin_low], 0)
    vis_copy.wait()
    rows = 2 * tiles
    for tile in range(tiles):
        parts = [vis[pl.ds(2 * tile + c, ticks, stride=rows), :] for c in range(2)]
        high, low = split(jnp.concatenate(parts, 1))
        product = mul(all_rows, high)
        product = product[: 2 * n] + product[2 * n :] + mul(high_rows, low)
        real = product[:n, :LANES] + product[n:, LANES:]
        imag = product[:n, LANES:] - product[n:, :LANES]
        spec_out[:, tile, :] = real
        spec_out[:, tiles + tile, :] = imag

    def send_spec(offset):
        pltpu.make_async_remote_copy(
            src_ref=spec_out.at[peer(offset)], dst_ref=spec_in.at[offset - 1],
            send_sem=spec_send, recv_sem=spec_recv,
            device_id={"ma": peer(offset)}, device_id_type=MESH,
        ).start()

    peers(send_spec)

    arrived = comp_in.at[pl.ds(0, n - 1)]
    pltpu.make_async_copy(arrived, arrived, comp_recv).wait()
    fields = [comp_in[:, row, :] for row in range(3)]
    if 2 * count == LANES and n % 2 == 0:
        fields = [jnp.concatenate([f[: n // 2, :count], f[n // 2 :, :count]], 1) for f in fields]
    index = fields[0] - me * width
    blocks = width // LANES
    row_id = lax.broadcasted_iota(jnp.int32, (2 * blocks, LANES), 0)
    low_id = lax.broadcasted_iota(jnp.int32, (LANES, LANES), 0)
    weights, places = [], []
    for chunk in range(index.shape[0]):
        at = index[chunk : chunk + 1]
        amp = jnp.where(
            (row_id & 1) == 1, fields[2][chunk : chunk + 1], fields[1][chunk : chunk + 1]
        )
        amp = jnp.where((at >> 7) == (row_id >> 1), amp, 0)
        halves = jnp.concatenate([amp >> 6, amp & 63], 0)
        weights.append(halves.astype(F32).astype(BF16))
        places.append(jnp.where((at & 127) == low_id, 1.0, 0.0).astype(BF16))
    halves = mul(jnp.concatenate(weights, 1), jnp.concatenate(places, 1), ((1,), (1,)))
    halves = halves.astype(jnp.int32)
    summed = halves[: 2 * blocks] * 64 + halves[2 * blocks :]
    model = summed.astype(F32) * (1.0 / 1024.0)
    model = jnp.concatenate([model[2 * i : 2 * i + 2] for i in range(blocks)], 1).astype(BF16)

    transfer_copy.wait()
    lines = tiles * LANES
    predicted = mul(model, transfer[...], ((1,), (1,)))
    pred_real = predicted[0:1, :lines] - predicted[1:2, lines:]
    pred_imag = predicted[1:2, :lines] + predicted[0:1, lines:]

    spec_in[n - 1] = spec_out[me]
    arrived = spec_in.at[pl.ds(0, n - 1)]
    pltpu.make_async_copy(arrived, arrived, spec_recv).wait()
    spectra = jnp.sum(spec_in[...], 0) * (1.0 / math.sqrt(ticks * n))
    real = jnp.concatenate([spectra[i : i + 1] for i in range(tiles)], 1)
    imag = jnp.concatenate([spectra[tiles + i : tiles + i + 1] for i in range(tiles)], 1)
    real, imag = real - pred_real, imag - pred_imag
    resid = jnp.concatenate(
        [jnp.concatenate([real, imag], 1), jnp.concatenate([imag, -real], 1)], 0
    ).astype(BF16)
    alm = mul(resid, transfer[...])
    for block in range(blocks):
        out_ref[2 * block : 2 * block + 2, :] = alm[:, block * LANES : (block + 1) * LANES]

    for buffer, sem in ((comp_in, comp_send), (spec_in, spec_send)):
        sent = buffer.at[pl.ds(0, n - 1)]
        pltpu.make_async_copy(sent, sent, sem).wait()


def body(vis, transfer, band_start, comp_index, comp_amp):
    n = lax.axis_size("ma")
    ticks, _, lines = vis.shape
    m_local, _, _, width = transfer.shape
    count = comp_index.shape[0]
    tiles = lines // LANES
    blocks = width // LANES
    assert m_local == 1 and lines % LANES == 0 and width % LANES == 0 and count <= LANES
    assert (ticks * n) & (ticks * n - 1) == 0
    flat_vis = (
        vis.reshape(ticks, 2, tiles, LANES).transpose(0, 2, 1, 3).reshape(ticks * 2 * tiles, LANES)
    )
    out = pl.pallas_call(
        functools.partial(kernel, n, ticks, tiles, count, width),
        out_shape=jax.ShapeDtypeStruct((2 * blocks, LANES), F32),
        in_specs=[
            pl.BlockSpec(memory_space=pl.ANY),
            pl.BlockSpec(memory_space=pl.ANY),
            pl.BlockSpec(memory_space=pltpu.SMEM),
            pl.BlockSpec(memory_space=pltpu.VMEM),
            pl.BlockSpec(memory_space=pltpu.VMEM),
        ],
        out_specs=pl.BlockSpec(memory_space=pltpu.VMEM),
        scratch_shapes=[
            pltpu.VMEM(flat_vis.shape, F32),
            pltpu.VMEM((2 * lines, width), BF16),
            pltpu.VMEM((4, LANES), jnp.int32),
            pltpu.VMEM((n, 4, LANES), jnp.int32),
            pltpu.VMEM((n, 2 * tiles, LANES), F32),
            pltpu.VMEM((n, 2 * tiles, LANES), F32),
        ]
        + [pltpu.SemaphoreType.DMA] * 6,
        compiler_params=pltpu.CompilerParams(
            collective_id=0, has_side_effects=True, vmem_limit_bytes=48 * 1024 * 1024
        ),
        cost_estimate=pl.CostEstimate(
            flops=2 * 2 * n * ticks * 2 * lines + 8 * lines * width * 2,
            bytes_accessed=vis.size * 4 + transfer.size * 2,
            transcendentals=0,
        ),
    )(
        flat_vis,
        transfer.reshape(2 * lines, width),
        band_start,
        comp_index.reshape(1, count),
        comp_amp.T,
    )
    return out.reshape(blocks, 2, LANES).transpose(1, 0, 2).reshape(1, 2, width)


def solution(mesh):
    in_specs = (
        P(("grp", "ma"), None, None),
        P(("grp", "ma"), None, None, None),
        P("grp"),
        P(("grp", "ma")),
        P(("grp", "ma"), None),
    )
    out_specs = P(("grp", "ma"), None, None)
    return jax.shard_map(body, mesh=mesh, in_specs=in_specs, out_specs=out_specs, check_vma=False)
```

time: 86.1 us -> 14.3 us (0.17)
  blocking collectives: 42.8 us -> 0 us
  starting transfers between devices: 10.9 us -> 0 us
  other arithmetic: 10.2 us -> 0 us
  Pallas kernels: 0 us -> 9.67 us
  waiting for transfers between devices: 6.28 us -> 0 us
  local copies, waits for them, and re-layouts: 9.1 us -> 3.72 us
  matrix products: 5.05 us -> 0 us
    unnamed x1 -> x0, blocking collectives: 23.3 us -> none
    all_gather x1 -> x0, blocking collectives: 19.4 us -> none  [body(): lax.all_gather(comp_amp, 'ma', axis=0, tiled=True)]
    all_to_all x2 -> x0, starting transfers between devices: 10.9 us -> none  [the longest x1 7.39 us: body(): lax.all_to_all(vis, 'ma', split_axis=2, concat_axis=0, tiled=True)]
    pallas_call x0 -> x1, Pallas kernels: none -> 9.67 us  [body(): pl.pallas_call(functools.partial(kernel, n, ticks, tiles, count, width),...]
    scatter-add x1 -> x0, other arithmetic: 7.26 us -> none  [body(): jax.ops.segment_sum(amp_all, target, num_segments=slots + 1)[:slots]]
    all_to_all x2 -> x0, waiting for transfers between devices: 6.28 us -> none  [the longest x1 6.28 us: body(): lax.all_to_all(local_spectra, 'ma', split_axis=0, concat_axis=2, tiled=True)]
    dot_general x3 -> x0, matrix products: 5.05 us -> none  [the longest x1 4.42 us: body(): jnp.dot(trig_pair, flat_visibility, precision=lax.Precision.HIGHEST, pref...]
    unnamed x15 -> x9, local copies, waits for them, and re-layouts: 7.42 us -> 3.72 us
  transfers between devices with their start and end apart: 2 -> 0, of which waited for: 1 -> 0; matrix products, arithmetic and copies ran while one was open for 13% -> 0% of each run, Pallas kernels for 0% -> 0%
where the time goes in v1:
time: 14.3 us; the launch traced here: 14.1 us
  Pallas kernels  9.67 us (68%)
  local copies, waits for them, and re-layouts  3.72 us (26%)
  between operations  0.68 us (5%)
    pallas_call x1, Pallas kernels, body(): pl.pallas_call(functools.partial(kernel, n, ticks, tiles, count, width),...  9.67 us
    unnamed x9, local copies, waits for them, and re-layouts  3.72 us

profile of v1, /device:TPU:0, one launch (start us, length us, event | category | flops | bytes accessed | tf_op | source)
XLA Modules:
  0.0 14.1 jit_solution(74812389028927556)
XLA Ops:
  0.7 0.0 copy-start.2
  0.7 0.0 copy-start.3
  0.7 0.7 %copy-done.2 = s32[64,2]{0,1:T(2,128)S(1)} copy-done((s32[64,2]{0,1:T(2,128)S(1)}, s32[64,2]{0,1:T(2,128)}, u32[]{:S(2)}) %copy-start.2) | copy-done | bytes 536
  1.3 0.0 copy-done.3
  1.3 0.0 copy-start
  1.3 1.2 %copy-done = f32[512,2,256]{2,1,0:T(2,128)S(1)} copy-done((f32[512,2,256]{2,1,0:T(2,128)S(1)}, f32[512,2,256]{2,1,0:T(2,128)}, u32[]{:S(2)}) %copy-start) | copy-done | bytes 1048600
  2.6 0.0 copy-start.1
  2.6 1.2 %copy-done.1 = bf16[1,2,256,1024]{3,2,1,0:T(8,128)(2,1)S(1)} copy-done((bf16[1,2,256,1024]{3,2,1,0:T(8,128)(2,1)S(1)}, bf16[1,2,256,1024]{3,2,1,0:T(8,128)(2,1)}, u32[]{:S(2)}) %copy-start.1) | copy-done | bytes 1048600
  3.8 9.7 %shard_map.55 = f32[16,128]{1,0:T(8,128)S(1)} custom-call(f32[2048,128]{1,0:T(8,128)S(1)} %bitcast.13, bf16[512,1024]{1,0:T(8,128)(2,1)S(1)} %bitcast.14, s32[1]{0:T(128)S(6)} %copy.9.start_ref, s32[1,64]{1,0:T(1,128)S(1)} %bitcast.17, s32[2,64]{1,0:T(2,128)S(1)} %bitcast.16), custom_call_target="tpu_custom_call" | custom-call | flops 20971520 | bytes 2097152 | tf_op jit(solution)/shard_map/pallas_call | solution.py:177
  13.5 0.6 %copy.10 = f32[1,2,1024]{2,1,0:T(2,128)} copy(f32[1,2,1024]{2,1,0:T(2,128)S(1)} %bitcast.15) | data formatting | bytes 16384
Async XLA Ops:
  0.7 0.7 %copy-start.2 = (s32[64,2]{0,1:T(2,128)S(1)}, s32[64,2]{0,1:T(2,128)}, u32[]{:S(2)}) copy-start(s32[64,2]{0,1:T(2,128)} %param.9) | copy-start | bytes 1540
  0.7 0.7 %copy-start.3 = (s32[64]{0:T(128)S(1)}, s32[64]{0:T(128)}, u32[]{:S(2)}) copy-start(s32[64]{0:T(128)} %param.8) | copy-start | bytes 772
  1.3 1.2 %copy-start = (f32[512,2,256]{2,1,0:T(2,128)S(1)}, f32[512,2,256]{2,1,0:T(2,128)}, u32[]{:S(2)}) copy-start(f32[512,2,256]{2,1,0:T(2,128)} %param.5) | copy-start | bytes 3145732
  2.6 1.2 %copy-start.1 = (bf16[1,2,256,1024]{3,2,1,0:T(8,128)(2,1)S(1)}, bf16[1,2,256,1024]{3,2,1,0:T(8,128)(2,1)}, u32[]{:S(2)}) copy-start(bf16[1,2,256,1024]{3,2,1,0:T(8,128)(2,1)} %param.6) | copy-start | bytes 3145732

commit v2 on v1

--- a/solution.py
+++ b/solution.py
@@ -44,15 +44,19 @@
 
 def kernel(
     n, ticks, tiles, count, width,
-    vis_hbm, transfer_hbm, start_ref, index_ref, amp_ref, out_ref,
-    vis, transfer, comp_out, comp_in, spec_out, spec_in,
-    vis_sem, transfer_sem, comp_send, comp_recv, spec_send, spec_recv,
+    vis_hbm, transfer_hbm, start_hbm, index_hbm, amp_hbm, out_ref,
+    vis, transfer, start_ref, index_ref, amp_ref, comp_out, comp_in, spec_out, spec_in,
+    vis_sem, transfer_sem, start_sem, index_sem, amp_sem,
+    comp_send, comp_recv, spec_send, spec_recv,
 ):
     me = lax.axis_index("ma")
+    start_copy = pltpu.make_async_copy(start_hbm, start_ref, start_sem)
+    index_copy = pltpu.make_async_copy(index_hbm, index_ref, index_sem)
+    amp_copy = pltpu.make_async_copy(amp_hbm, amp_ref, amp_sem)
     vis_copy = pltpu.make_async_copy(vis_hbm, vis, vis_sem)
     transfer_copy = pltpu.make_async_copy(transfer_hbm, transfer, transfer_sem)
-    vis_copy.start()
-    transfer_copy.start()
+    for copy in (start_copy, index_copy, amp_copy, vis_copy, transfer_copy):
+        copy.start()
 
     def peers(step):
         if n <= 32:
@@ -73,9 +77,16 @@
     peers(greet)
 
     comp_out[...] = jnp.full(comp_out.shape, -1, jnp.int32)
+    index_copy.wait()
+    amp_copy.wait()
     comp_out[0:1, 0:count] = index_ref[...]
     comp_out[1:3, 0:count] = amp_ref[...]
     comp_in[n - 1] = comp_out[...]
+    start_copy.wait()
+    cos, sin = trig_pair(start_ref[...], me * ticks, n, ticks, ticks * n)
+    (cos_high, cos_low), (sin_high, sin_low) = split(cos), split(sin)
+    high_rows = jnp.concatenate([cos_high, sin_high], 0)
+    all_rows = jnp.concatenate([cos_high, sin_high, cos_low, sin_low], 0)
     pl.semaphore_wait(barrier, n - 1)
 
     def send_comp(offset):
@@ -87,10 +98,6 @@
 
     peers(send_comp)
 
-    cos, sin = trig_pair(start_ref[0], me * ticks, n, ticks, ticks * n)
-    (cos_high, cos_low), (sin_high, sin_low) = split(cos), split(sin)
-    high_rows = jnp.concatenate([cos_high, sin_high], 0)
-    all_rows = jnp.concatenate([cos_high, sin_high, cos_low, sin_low], 0)
     vis_copy.wait()
     rows = 2 * tiles
     for tile in range(tiles):
@@ -178,24 +185,24 @@
         functools.partial(kernel, n, ticks, tiles, count, width),
         out_shape=jax.ShapeDtypeStruct((2 * blocks, LANES), F32),
         in_specs=[
-            pl.BlockSpec(memory_space=pl.ANY),
-            pl.BlockSpec(memory_space=pl.ANY),
-            pl.BlockSpec(memory_space=pltpu.SMEM),
-            pl.BlockSpec(memory_space=pltpu.VMEM),
-            pl.BlockSpec(memory_space=pltpu.VMEM),
-        ],
+            pl.BlockSpec(memory_space=pltpu.HBM),
+        ]
+        * 5,
         out_specs=pl.BlockSpec(memory_space=pltpu.VMEM),
         scratch_shapes=[
             pltpu.VMEM(flat_vis.shape, F32),
             pltpu.VMEM((2 * lines, width), BF16),
+            pltpu.VMEM((1, 1), jnp.int32),
+            pltpu.VMEM((1, count), jnp.int32),
+            pltpu.VMEM((2, count), jnp.int32),
             pltpu.VMEM((4, LANES), jnp.int32),
             pltpu.VMEM((n, 4, LANES), jnp.int32),
             pltpu.VMEM((n, 2 * tiles, LANES), F32),
             pltpu.VMEM((n, 2 * tiles, LANES), F32),
         ]
-        + [pltpu.SemaphoreType.DMA] * 6,
+        + [pltpu.SemaphoreType.DMA] * 9,
         compiler_params=pltpu.CompilerParams(
-            collective_id=0, has_side_effects=True, vmem_limit_bytes=48 * 1024 * 1024
+            collective_id=0, has_side_effects=True, vmem_limit_bytes=64 * 1024 * 1024
         ),
         cost_estimate=pl.CostEstimate(
             flops=2 * 2 * n * ticks * 2 * lines + 8 * lines * width * 2,
@@ -205,7 +212,7 @@
     )(
         flat_vis,
         transfer.reshape(2 * lines, width),
-        band_start,
+        band_start.reshape(1, 1),
         comp_index.reshape(1, count),
         comp_amp.T,
     )

time: 14.3 us -> 12.5 us (0.87)
  local copies, waits for them, and re-layouts: 3.72 us -> 1.3 us
  Pallas kernels: 9.67 us -> 10.3 us
    unnamed x9 -> x1, local copies, waits for them, and re-layouts: 3.72 us -> 1.3 us
    pallas_call x1, Pallas kernels: 9.67 us -> 10.3 us  [body(): pl.pallas_call(functools.partial(kernel, n, ticks, tiles, count, width),...]
where the time goes in v2:
time: 12.5 us; the launch traced here: 12.3 us
  Pallas kernels  10.3 us (82%)
  local copies, waits for them, and re-layouts  1.3 us (10%)
  between operations  0.66 us (5%)
    pallas_call x1, Pallas kernels, body(): pl.pallas_call(functools.partial(kernel, n, ticks, tiles, count, width),...  10.3 us
    unnamed x1, local copies, waits for them, and re-layouts  1.3 us

profile of v2, /device:TPU:0, one launch (start us, length us, event | category | flops | bytes accessed | tf_op | source)
XLA Modules:
  0.0 12.3 jit_solution(2465385041592755663)
XLA Ops:
  0.7 10.3 %shard_map.55 = f32[16,128]{1,0:T(8,128)} custom-call(f32[2048,128]{1,0:T(8,128)} %bitcast.15, bf16[512,1024]{1,0:T(8,128)(2,1)} %bitcast.16, s32[1,1]{1,0:T(1,128)} %bitcast.14.start_hbm, s32[1,64]{1,0:T(1,128)} %bitcast.19, s32[2,64]{1,0:T(2,128)} %bitcast.18), custom_call_target="tpu_custom_call" | custom-call | flops 20971520 | bytes 2097152 | tf_op jit(solution)/shard_map/pallas_call | solution.py:184
  11.0 1.3 %copy.10 = f32[1,2,1024]{2,1,0:T(2,128)} copy(f32[1,2,1024]{2,1,0:T(2,128)} %bitcast.17) | data formatting | bytes 16384

commit v3 on v2

--- a/solution.py
+++ b/solution.py
@@ -44,18 +44,17 @@
 
 def kernel(
     n, ticks, tiles, count, width,
-    vis_hbm, transfer_hbm, start_hbm, index_hbm, amp_hbm, out_ref,
-    vis, transfer, start_ref, index_ref, amp_ref, comp_out, comp_in, spec_out, spec_in,
-    vis_sem, transfer_sem, start_sem, index_sem, amp_sem,
+    start_ref, vis_hbm, transfer_hbm, index_hbm, amp_hbm, out_ref,
+    vis, transfer, index_ref, amp_ref, comp_out, comp_in, spec_out, spec_in,
+    vis_sem, transfer_sem, index_sem, amp_sem,
     comp_send, comp_recv, spec_send, spec_recv,
 ):
     me = lax.axis_index("ma")
-    start_copy = pltpu.make_async_copy(start_hbm, start_ref, start_sem)
     index_copy = pltpu.make_async_copy(index_hbm, index_ref, index_sem)
     amp_copy = pltpu.make_async_copy(amp_hbm, amp_ref, amp_sem)
     vis_copy = pltpu.make_async_copy(vis_hbm, vis, vis_sem)
     transfer_copy = pltpu.make_async_copy(transfer_hbm, transfer, transfer_sem)
-    for copy in (start_copy, index_copy, amp_copy, vis_copy, transfer_copy):
+    for copy in (index_copy, amp_copy, vis_copy, transfer_copy):
         copy.start()
 
     def peers(step):
@@ -82,8 +81,7 @@
     comp_out[0:1, 0:count] = index_ref[...]
     comp_out[1:3, 0:count] = amp_ref[...]
     comp_in[n - 1] = comp_out[...]
-    start_copy.wait()
-    cos, sin = trig_pair(start_ref[...], me * ticks, n, ticks, ticks * n)
+    cos, sin = trig_pair(start_ref[0], me * ticks, n, ticks, ticks * n)
     (cos_high, cos_low), (sin_high, sin_low) = split(cos), split(sin)
     high_rows = jnp.concatenate([cos_high, sin_high], 0)
     all_rows = jnp.concatenate([cos_high, sin_high, cos_low, sin_low], 0)
@@ -183,16 +181,15 @@
     )
     out = pl.pallas_call(
         functools.partial(kernel, n, ticks, tiles, count, width),
-        out_shape=jax.ShapeDtypeStruct((2 * blocks, LANES), F32),
+        out_shape=pltpu.VMEM((2 * blocks, LANES), F32),
         in_specs=[
-            pl.BlockSpec(memory_space=pltpu.HBM),
+            pl.BlockSpec(memory_space=pltpu.SMEM),
         ]
-        * 5,
+        + [pl.BlockSpec(memory_space=pltpu.HBM)] * 4,
         out_specs=pl.BlockSpec(memory_space=pltpu.VMEM),
         scratch_shapes=[
             pltpu.VMEM(flat_vis.shape, F32),
             pltpu.VMEM((2 * lines, width), BF16),
-            pltpu.VMEM((1, 1), jnp.int32),
             pltpu.VMEM((1, count), jnp.int32),
             pltpu.VMEM((2, count), jnp.int32),
             pltpu.VMEM((4, LANES), jnp.int32),
@@ -200,9 +197,9 @@
             pltpu.VMEM((n, 2 * tiles, LANES), F32),
             pltpu.VMEM((n, 2 * tiles, LANES), F32),
         ]
-        + [pltpu.SemaphoreType.DMA] * 9,
+        + [pltpu.SemaphoreType.DMA] * 8,
         compiler_params=pltpu.CompilerParams(
-            collective_id=0, has_side_effects=True, vmem_limit_bytes=64 * 1024 * 1024
+            collective_id=0, has_side_effects=True, vmem_limit_bytes=40 * 1024 * 1024
         ),
         cost_estimate=pl.CostEstimate(
             flops=2 * 2 * n * ticks * 2 * lines + 8 * lines * width * 2,
@@ -210,11 +207,16 @@
             transcendentals=0,
         ),
     )(
-        flat_vis,
-        transfer.reshape(2 * lines, width),
-        band_start.reshape(1, 1),
-        comp_index.reshape(1, count),
-        comp_amp.T,
+        band_start,
+        *(
+            pltpu.with_memory_space_constraint(operand, pltpu.HBM)
+            for operand in (
+                flat_vis,
+                transfer.reshape(2 * lines, width),
+                comp_index.reshape(1, count),
+                comp_amp.T,
+            )
+        ),
     )
     return out.reshape(blocks, 2, LANES).transpose(1, 0, 2).reshape(1, 2, width)
 

time: 12.5 us -> 11 us (0.88); the launches traced: 12.3 us -> 10.9 us
  local copies, waits for them, and re-layouts: 1.3 us -> 0.6 us
  Pallas kernels: 10.3 us -> 9.63 us
    unnamed x1, local copies, waits for them, and re-layouts: 1.3 us -> 0.6 us
    pallas_call x1, Pallas kernels: 10.3 us -> 9.63 us  [body(): pl.pallas_call(functools.partial(kernel, n, ticks, tiles, count, width),...]
where the time goes in v3:
time: 11 us; the launch traced here: 10.9 us
  Pallas kernels  9.63 us (88%)
  between operations  0.66 us (6%)
  local copies, waits for them, and re-layouts  0.6 us (5%)
    pallas_call x1, Pallas kernels, body(): pl.pallas_call(functools.partial(kernel, n, ticks, tiles, count, width),...  9.63 us
    unnamed x1, local copies, waits for them, and re-layouts  0.6 us

profile of v3, /device:TPU:0, one launch (start us, length us, event | category | flops | bytes accessed | tf_op | source)
XLA Modules:
  0.0 10.9 jit_solution(15721901934559723283)
XLA Ops:
  0.7 9.6 %shard_map.55 = f32[16,128]{1,0:T(8,128)S(1)} custom-call(s32[1]{0:T(128)S(6)} %copy.10.start_ref, f32[2048,128]{1,0:T(8,128)} %bitcast.14, bf16[512,1024]{1,0:T(8,128)(2,1)} %bitcast.15, s32[1,64]{1,0:T(1,128)} %bitcast.17, s32[2,64]{1,0:T(2,128)} %bitcast.16), custom_call_target="tpu_custom_call" | custom-call | flops 20971520 | bytes 2097152 | tf_op jit(solution)/shard_map/pallas_call | solution.py:182
  10.3 0.6 %copy.9 = f32[1,2,1024]{2,1,0:T(2,128)} copy(f32[1,2,1024]{2,1,0:T(2,128)S(1)} %bitcast.13) | data formatting | bytes 16384

commit v4 on v3

--- a/solution.py
+++ b/solution.py
@@ -43,18 +43,22 @@
 
 
 def kernel(
-    n, ticks, tiles, count, width,
+    n, ticks, tiles, count, width, rows, pieces,
     start_ref, vis_hbm, transfer_hbm, index_hbm, amp_hbm, out_ref,
-    vis, transfer, index_ref, amp_ref, comp_out, comp_in, spec_out, spec_in,
-    vis_sem, transfer_sem, index_sem, amp_sem,
-    comp_send, comp_recv, spec_send, spec_recv,
+    vis, transfer, index_ref, amp_ref, outgoing, incoming,
+    vis_sem, transfer_sem, index_sem, amp_sem, send_sem, recv_sem,
 ):
     me = lax.axis_index("ma")
+    spec_rows = 2 * tiles
     index_copy = pltpu.make_async_copy(index_hbm, index_ref, index_sem)
     amp_copy = pltpu.make_async_copy(amp_hbm, amp_ref, amp_sem)
-    vis_copy = pltpu.make_async_copy(vis_hbm, vis, vis_sem)
+    piece = ticks * spec_rows // pieces
+    vis_copies = []
+    for i in range(pieces):
+        part = pl.ds(i * piece, piece)
+        vis_copies.append(pltpu.make_async_copy(vis_hbm.at[part], vis.at[part], vis_sem.at[i]))
     transfer_copy = pltpu.make_async_copy(transfer_hbm, transfer, transfer_sem)
-    for copy in (index_copy, amp_copy, vis_copy, transfer_copy):
+    for copy in (*vis_copies, index_copy, amp_copy, transfer_copy):
         copy.start()
 
     def peers(step):
@@ -68,6 +72,9 @@
         target = me + offset
         return jnp.where(target >= n, target - n, target)
 
+    def slot(index):
+        return pl.ds(pl.multiple_of(index * rows, rows), rows)
+
     barrier = pltpu.get_barrier_semaphore()
 
     def greet(offset):
@@ -75,51 +82,53 @@
 
     peers(greet)
 
-    comp_out[...] = jnp.full(comp_out.shape, -1, jnp.int32)
-    index_copy.wait()
-    amp_copy.wait()
-    comp_out[0:1, 0:count] = index_ref[...]
-    comp_out[1:3, 0:count] = amp_ref[...]
-    comp_in[n - 1] = comp_out[...]
     cos, sin = trig_pair(start_ref[0], me * ticks, n, ticks, ticks * n)
     (cos_high, cos_low), (sin_high, sin_low) = split(cos), split(sin)
     high_rows = jnp.concatenate([cos_high, sin_high], 0)
     all_rows = jnp.concatenate([cos_high, sin_high, cos_low, sin_low], 0)
-    pl.semaphore_wait(barrier, n - 1)
-
-    def send_comp(offset):
-        pltpu.make_async_remote_copy(
-            src_ref=comp_out, dst_ref=comp_in.at[offset - 1],
-            send_sem=comp_send, recv_sem=comp_recv,
-            device_id={"ma": peer(offset)}, device_id_type=MESH,
-        ).start()
-
-    peers(send_comp)
-
-    vis_copy.wait()
-    rows = 2 * tiles
+
+    index_copy.wait()
+    amp_copy.wait()
+    fields = [index_ref[...], amp_ref[0:1], amp_ref[1:2]]
+    for row in range(spec_rows, rows):
+        if row < spec_rows + 3:
+            field = fields[row - spec_rows].astype(F32)
+            if count < LANES:
+                field = jnp.concatenate([field, jnp.full((1, LANES - count), -1.0, F32)], 1)
+        else:
+            field = jnp.zeros((1, LANES), F32)
+        outgoing[pl.ds(row, n, stride=rows), :] = jnp.broadcast_to(field, (n, LANES))
+
+    for copy in vis_copies:
+        copy.wait()
     for tile in range(tiles):
-        parts = [vis[pl.ds(2 * tile + c, ticks, stride=rows), :] for c in range(2)]
+        parts = [vis[pl.ds(2 * tile + c, ticks, stride=spec_rows), :] for c in range(2)]
         high, low = split(jnp.concatenate(parts, 1))
         product = mul(all_rows, high)
         product = product[: 2 * n] + product[2 * n :] + mul(high_rows, low)
         real = product[:n, :LANES] + product[n:, LANES:]
         imag = product[:n, LANES:] - product[n:, :LANES]
-        spec_out[:, tile, :] = real
-        spec_out[:, tiles + tile, :] = imag
-
-    def send_spec(offset):
+        outgoing[pl.ds(tile, n, stride=rows), :] = real
+        outgoing[pl.ds(tiles + tile, n, stride=rows), :] = imag
+
+    pl.semaphore_wait(barrier, n - 1)
+
+    def send(offset):
         pltpu.make_async_remote_copy(
-            src_ref=spec_out.at[peer(offset)], dst_ref=spec_in.at[offset - 1],
-            send_sem=spec_send, recv_sem=spec_recv,
+            src_ref=outgoing.at[slot(peer(offset))], dst_ref=incoming.at[slot(offset - 1)],
+            send_sem=send_sem, recv_sem=recv_sem,
             device_id={"ma": peer(offset)}, device_id_type=MESH,
         ).start()
 
-    peers(send_spec)
-
-    arrived = comp_in.at[pl.ds(0, n - 1)]
-    pltpu.make_async_copy(arrived, arrived, comp_recv).wait()
-    fields = [comp_in[:, row, :] for row in range(3)]
+    peers(send)
+    incoming[slot(n - 1), :] = outgoing[slot(me), :]
+    transfer_copy.wait()
+    arrived = incoming.at[pl.ds(0, (n - 1) * rows)]
+    pltpu.make_async_copy(arrived, arrived, recv_sem).wait()
+
+    fields = [
+        incoming[pl.ds(spec_rows + row, n, stride=rows), :].astype(jnp.int32) for row in range(3)
+    ]
     if 2 * count == LANES and n % 2 == 0:
         fields = [jnp.concatenate([f[: n // 2, :count], f[n // 2 :, :count]], 1) for f in fields]
     index = fields[0] - me * width
@@ -142,16 +151,12 @@
     model = summed.astype(F32) * (1.0 / 1024.0)
     model = jnp.concatenate([model[2 * i : 2 * i + 2] for i in range(blocks)], 1).astype(BF16)
 
-    transfer_copy.wait()
     lines = tiles * LANES
     predicted = mul(model, transfer[...], ((1,), (1,)))
     pred_real = predicted[0:1, :lines] - predicted[1:2, lines:]
     pred_imag = predicted[1:2, :lines] + predicted[0:1, lines:]
 
-    spec_in[n - 1] = spec_out[me]
-    arrived = spec_in.at[pl.ds(0, n - 1)]
-    pltpu.make_async_copy(arrived, arrived, spec_recv).wait()
-    spectra = jnp.sum(spec_in[...], 0) * (1.0 / math.sqrt(ticks * n))
+    spectra = jnp.sum(incoming[...].reshape(n, rows, LANES), 0) * (1.0 / math.sqrt(ticks * n))
     real = jnp.concatenate([spectra[i : i + 1] for i in range(tiles)], 1)
     imag = jnp.concatenate([spectra[tiles + i : tiles + i + 1] for i in range(tiles)], 1)
     real, imag = real - pred_real, imag - pred_imag
@@ -162,9 +167,7 @@
     for block in range(blocks):
         out_ref[2 * block : 2 * block + 2, :] = alm[:, block * LANES : (block + 1) * LANES]
 
-    for buffer, sem in ((comp_in, comp_send), (spec_in, spec_send)):
-        sent = buffer.at[pl.ds(0, n - 1)]
-        pltpu.make_async_copy(sent, sent, sem).wait()
+    pltpu.make_async_copy(arrived, arrived, send_sem).wait()
 
 
 def body(vis, transfer, band_start, comp_index, comp_amp):
@@ -175,12 +178,15 @@
     tiles = lines // LANES
     blocks = width // LANES
     assert m_local == 1 and lines % LANES == 0 and width % LANES == 0 and count <= LANES
+    rows = -(-(2 * tiles + 3) // 8) * 8
+    pieces = 4
+    assert ticks * 2 * tiles % (8 * pieces) == 0
     assert (ticks * n) & (ticks * n - 1) == 0
     flat_vis = (
         vis.reshape(ticks, 2, tiles, LANES).transpose(0, 2, 1, 3).reshape(ticks * 2 * tiles, LANES)
     )
     out = pl.pallas_call(
-        functools.partial(kernel, n, ticks, tiles, count, width),
+        functools.partial(kernel, n, ticks, tiles, count, width, rows, pieces),
         out_shape=pltpu.VMEM((2 * blocks, LANES), F32),
         in_specs=[
             pl.BlockSpec(memory_space=pltpu.SMEM),
@@ -192,12 +198,11 @@
             pltpu.VMEM((2 * lines, width), BF16),
             pltpu.VMEM((1, count), jnp.int32),
             pltpu.VMEM((2, count), jnp.int32),
-            pltpu.VMEM((4, LANES), jnp.int32),
-            pltpu.VMEM((n, 4, LANES), jnp.int32),
-            pltpu.VMEM((n, 2 * tiles, LANES), F32),
-            pltpu.VMEM((n, 2 * tiles, LANES), F32),
+            pltpu.VMEM((n * rows, LANES), F32),
+            pltpu.VMEM((n * rows, LANES), F32),
+            pltpu.SemaphoreType.DMA((pieces,)),
         ]
-        + [pltpu.SemaphoreType.DMA] * 8,
+        + [pltpu.SemaphoreType.DMA] * 5,
         compiler_params=pltpu.CompilerParams(
             collective_id=0, has_side_effects=True, vmem_limit_bytes=40 * 1024 * 1024
         ),

time: 11 us -> 11.6 us (1.055)
  Pallas kernels: 9.63 us -> 10.2 us
    pallas_call x1, Pallas kernels: 9.63 us -> 10.2 us  [body(): pl.pallas_call(functools.partial(kernel, n, ticks, tiles, count, width, r...]
where the time goes in v4:
time: 11.6 us; the launch traced here: 11.4 us
  Pallas kernels  10.2 us (88%)
  between operations  0.66 us (6%)
  local copies, waits for them, and re-layouts  0.6 us (5%)
    pallas_call x1, Pallas kernels, body(): pl.pallas_call(functools.partial(kernel, n, ticks, tiles, count, width, r...  10.2 us
    unnamed x1, local copies, waits for them, and re-layouts  0.6 us

profile of v4, /device:TPU:0, one launch (start us, length us, event | category | flops | bytes accessed | tf_op | source)
XLA Modules:
  0.0 11.4 jit_solution(4439390994149240405)
XLA Ops:
  0.7 10.2 %shard_map.55 = f32[16,128]{1,0:T(8,128)S(1)} custom-call(s32[1]{0:T(128)S(6)} %copy.10.start_ref, f32[2048,128]{1,0:T(8,128)} %bitcast.14, bf16[512,1024]{1,0:T(8,128)(2,1)} %bitcast.15, s32[1,64]{1,0:T(1,128)} %bitcast.17, s32[2,64]{1,0:T(2,128)} %bitcast.16), custom_call_target="tpu_custom_call" | custom-call | flops 20971520 | bytes 2097152 | tf_op jit(solution)/shard_map/pallas_call | solution.py:188
  10.8 0.6 %copy.9 = f32[1,2,1024]{2,1,0:T(2,128)} copy(f32[1,2,1024]{2,1,0:T(2,128)S(1)} %bitcast.13) | data formatting | bytes 16384

commit v5 on v3

--- a/solution.py
+++ b/solution.py
@@ -43,7 +43,7 @@
 
 
 def kernel(
-    n, ticks, tiles, count, width,
+    n, ticks, tiles, count, width, pieces,
     start_ref, vis_hbm, transfer_hbm, index_hbm, amp_hbm, out_ref,
     vis, transfer, index_ref, amp_ref, comp_out, comp_in, spec_out, spec_in,
     vis_sem, transfer_sem, index_sem, amp_sem,
@@ -52,9 +52,13 @@
     me = lax.axis_index("ma")
     index_copy = pltpu.make_async_copy(index_hbm, index_ref, index_sem)
     amp_copy = pltpu.make_async_copy(amp_hbm, amp_ref, amp_sem)
-    vis_copy = pltpu.make_async_copy(vis_hbm, vis, vis_sem)
+    piece = vis.shape[0] // pieces
+    vis_copies = []
+    for i in range(pieces):
+        part = pl.ds(i * piece, piece)
+        vis_copies.append(pltpu.make_async_copy(vis_hbm.at[part], vis.at[part], vis_sem.at[i]))
     transfer_copy = pltpu.make_async_copy(transfer_hbm, transfer, transfer_sem)
-    for copy in (index_copy, amp_copy, vis_copy, transfer_copy):
+    for copy in (*vis_copies, index_copy, amp_copy, transfer_copy):
         copy.start()
 
     def peers(step):
@@ -85,18 +89,8 @@
     (cos_high, cos_low), (sin_high, sin_low) = split(cos), split(sin)
     high_rows = jnp.concatenate([cos_high, sin_high], 0)
     all_rows = jnp.concatenate([cos_high, sin_high, cos_low, sin_low], 0)
-    pl.semaphore_wait(barrier, n - 1)
-
-    def send_comp(offset):
-        pltpu.make_async_remote_copy(
-            src_ref=comp_out, dst_ref=comp_in.at[offset - 1],
-            send_sem=comp_send, recv_sem=comp_recv,
-            device_id={"ma": peer(offset)}, device_id_type=MESH,
-        ).start()
-
-    peers(send_comp)
-
-    vis_copy.wait()
+    for copy in vis_copies:
+        copy.wait()
     rows = 2 * tiles
     for tile in range(tiles):
         parts = [vis[pl.ds(2 * tile + c, ticks, stride=rows), :] for c in range(2)]
@@ -107,6 +101,17 @@
         imag = product[:n, LANES:] - product[n:, :LANES]
         spec_out[:, tile, :] = real
         spec_out[:, tiles + tile, :] = imag
+
+    pl.semaphore_wait(barrier, n - 1)
+
+    def send_comp(offset):
+        pltpu.make_async_remote_copy(
+            src_ref=comp_out, dst_ref=comp_in.at[offset - 1],
+            send_sem=comp_send, recv_sem=comp_recv,
+            device_id={"ma": peer(offset)}, device_id_type=MESH,
+        ).start()
+
+    peers(send_comp)
 
     def send_spec(offset):
         pltpu.make_async_remote_copy(
@@ -175,12 +180,14 @@
     tiles = lines // LANES
     blocks = width // LANES
     assert m_local == 1 and lines % LANES == 0 and width % LANES == 0 and count <= LANES
+    pieces = 4
+    assert ticks * 2 * tiles % (8 * pieces) == 0
     assert (ticks * n) & (ticks * n - 1) == 0
     flat_vis = (
         vis.reshape(ticks, 2, tiles, LANES).transpose(0, 2, 1, 3).reshape(ticks * 2 * tiles, LANES)
     )
     out = pl.pallas_call(
-        functools.partial(kernel, n, ticks, tiles, count, width),
+        functools.partial(kernel, n, ticks, tiles, count, width, pieces),
         out_shape=pltpu.VMEM((2 * blocks, LANES), F32),
         in_specs=[
             pl.BlockSpec(memory_space=pltpu.SMEM),
@@ -197,7 +204,8 @@
             pltpu.VMEM((n, 2 * tiles, LANES), F32),
             pltpu.VMEM((n, 2 * tiles, LANES), F32),
         ]
-        + [pltpu.SemaphoreType.DMA] * 8,
+        + [pltpu.SemaphoreType.DMA((pieces,))]
+        + [pltpu.SemaphoreType.DMA] * 7,
         compiler_params=pltpu.CompilerParams(
             collective_id=0, has_side_effects=True, vmem_limit_bytes=40 * 1024 * 1024
         ),

time: 11 us -> 11.7 us (1.064)
  Pallas kernels: 9.63 us -> 10.3 us
    pallas_call x1, Pallas kernels: 9.63 us -> 10.3 us  [body(): pl.pallas_call(functools.partial(kernel, n, ticks, tiles, count, width, p...]
where the time goes in v5:
time: 11.7 us; the launch traced here: 11.5 us
  Pallas kernels  10.3 us (88%)
  between operations  0.66 us (6%)
  local copies, waits for them, and re-layouts  0.6 us (5%)
    pallas_call x1, Pallas kernels, body(): pl.pallas_call(functools.partial(kernel, n, ticks, tiles, count, width, p...  10.3 us
    unnamed x1, local copies, waits for them, and re-layouts  0.6 us

profile of v5, /device:TPU:0, one launch (start us, length us, event | category | flops | bytes accessed | tf_op | source)
XLA Modules:
  0.0 11.5 jit_solution(9950318374119781288)
XLA Ops:
  0.7 10.3 %shard_map.55 = f32[16,128]{1,0:T(8,128)S(1)} custom-call(s32[1]{0:T(128)S(6)} %copy.10.start_ref, f32[2048,128]{1,0:T(8,128)} %bitcast.14, bf16[512,1024]{1,0:T(8,128)(2,1)} %bitcast.15, s32[1,64]{1,0:T(1,128)} %bitcast.17, s32[2,64]{1,0:T(2,128)} %bitcast.16), custom_call_target="tpu_custom_call" | custom-call | flops 20971520 | bytes 2097152 | tf_op jit(solution)/shard_map/pallas_call | solution.py:189
  10.9 0.6 %copy.9 = f32[1,2,1024]{2,1,0:T(2,128)} copy(f32[1,2,1024]{2,1,0:T(2,128)S(1)} %bitcast.13) | data formatting | bytes 16384

commit v6 on v5

--- a/solution.py
+++ b/solution.py
@@ -58,7 +58,7 @@
         part = pl.ds(i * piece, piece)
         vis_copies.append(pltpu.make_async_copy(vis_hbm.at[part], vis.at[part], vis_sem.at[i]))
     transfer_copy = pltpu.make_async_copy(transfer_hbm, transfer, transfer_sem)
-    for copy in (*vis_copies, index_copy, amp_copy, transfer_copy):
+    for copy in (index_copy, amp_copy, *vis_copies, transfer_copy):
         copy.start()
 
     def peers(step):
@@ -79,16 +79,28 @@
 
     peers(greet)
 
+    cos, sin = trig_pair(start_ref[0], me * ticks, n, ticks, ticks * n)
+    (cos_high, cos_low), (sin_high, sin_low) = split(cos), split(sin)
+    high_rows = jnp.concatenate([cos_high, sin_high], 0)
+    all_rows = jnp.concatenate([cos_high, sin_high, cos_low, sin_low], 0)
+
     comp_out[...] = jnp.full(comp_out.shape, -1, jnp.int32)
     index_copy.wait()
     amp_copy.wait()
     comp_out[0:1, 0:count] = index_ref[...]
     comp_out[1:3, 0:count] = amp_ref[...]
     comp_in[n - 1] = comp_out[...]
-    cos, sin = trig_pair(start_ref[0], me * ticks, n, ticks, ticks * n)
-    (cos_high, cos_low), (sin_high, sin_low) = split(cos), split(sin)
-    high_rows = jnp.concatenate([cos_high, sin_high], 0)
-    all_rows = jnp.concatenate([cos_high, sin_high, cos_low, sin_low], 0)
+    pl.semaphore_wait(barrier, n - 1)
+
+    def send_comp(offset):
+        pltpu.make_async_remote_copy(
+            src_ref=comp_out, dst_ref=comp_in.at[offset - 1],
+            send_sem=comp_send, recv_sem=comp_recv,
+            device_id={"ma": peer(offset)}, device_id_type=MESH,
+        ).start()
+
+    peers(send_comp)
+
     for copy in vis_copies:
         copy.wait()
     rows = 2 * tiles
@@ -101,17 +113,6 @@
         imag = product[:n, LANES:] - product[n:, :LANES]
         spec_out[:, tile, :] = real
         spec_out[:, tiles + tile, :] = imag
-
-    pl.semaphore_wait(barrier, n - 1)
-
-    def send_comp(offset):
-        pltpu.make_async_remote_copy(
-            src_ref=comp_out, dst_ref=comp_in.at[offset - 1],
-            send_sem=comp_send, recv_sem=comp_recv,
-            device_id={"ma": peer(offset)}, device_id_type=MESH,
-        ).start()
-
-    peers(send_comp)
 
     def send_spec(offset):
         pltpu.make_async_remote_copy(

time: 11.7 us -> 11.1 us (0.949)
  Pallas kernels: 10.3 us -> 9.71 us
    pallas_call x1, Pallas kernels: 10.3 us -> 9.71 us  [body(): pl.pallas_call(functools.partial(kernel, n, ticks, tiles, count, width, p...]
where the time goes in v6:
time: 11.1 us; the launch traced here: 11 us
  Pallas kernels  9.71 us (87%)
  between operations  0.66 us (6%)
  local copies, waits for them, and re-layouts  0.6 us (5%)
    pallas_call x1, Pallas kernels, body(): pl.pallas_call(functools.partial(kernel, n, ticks, tiles, count, width, p...  9.71 us
    unnamed x1, local copies, waits for them, and re-layouts  0.6 us

profile of v6, /device:TPU:0, one launch (start us, length us, event | category | flops | bytes accessed | tf_op | source)
XLA Modules:
  0.0 11.0 jit_solution(2836148077845584837)
XLA Ops:
  0.7 9.7 %shard_map.55 = f32[16,128]{1,0:T(8,128)S(1)} custom-call(s32[1]{0:T(128)S(6)} %copy.10.start_ref, f32[2048,128]{1,0:T(8,128)} %bitcast.14, bf16[512,1024]{1,0:T(8,128)(2,1)} %bitcast.15, s32[1,64]{1,0:T(1,128)} %bitcast.17, s32[2,64]{1,0:T(2,128)} %bitcast.16), custom_call_target="tpu_custom_call" | custom-call | flops 20971520 | bytes 2097152 | tf_op jit(solution)/shard_map/pallas_call | solution.py:190
  10.4 0.6 %copy.9 = f32[1,2,1024]{2,1,0:T(2,128)} copy(f32[1,2,1024]{2,1,0:T(2,128)S(1)} %bitcast.13) | data formatting | bytes 16384

commit v7 on v6

--- a/solution.py
+++ b/solution.py
@@ -58,8 +58,6 @@
         part = pl.ds(i * piece, piece)
         vis_copies.append(pltpu.make_async_copy(vis_hbm.at[part], vis.at[part], vis_sem.at[i]))
     transfer_copy = pltpu.make_async_copy(transfer_hbm, transfer, transfer_sem)
-    for copy in (index_copy, amp_copy, *vis_copies, transfer_copy):
-        copy.start()
 
     def peers(step):
         if n <= 32:
@@ -78,6 +76,8 @@
         pl.semaphore_signal(barrier, inc=1, device_id={"ma": peer(offset)}, device_id_type=MESH)
 
     peers(greet)
+    for copy in (index_copy, amp_copy, *vis_copies, transfer_copy):
+        copy.start()
 
     cos, sin = trig_pair(start_ref[0], me * ticks, n, ticks, ticks * n)
     (cos_high, cos_low), (sin_high, sin_low) = split(cos), split(sin)
@@ -90,6 +90,20 @@
     comp_out[0:1, 0:count] = index_ref[...]
     comp_out[1:3, 0:count] = amp_ref[...]
     comp_in[n - 1] = comp_out[...]
+    def transform(some_tiles):
+        for tile in some_tiles:
+            parts = [vis[pl.ds(2 * tile + c, ticks, stride=2 * tiles), :] for c in range(2)]
+            high, low = split(jnp.concatenate(parts, 1))
+            product = mul(all_rows, high)
+            product = product[: 2 * n] + product[2 * n :] + mul(high_rows, low)
+            real = product[:n, :LANES] + product[n:, LANES:]
+            imag = product[:n, LANES:] - product[n:, :LANES]
+            spec_out[:, tile, :] = real
+            spec_out[:, tiles + tile, :] = imag
+
+    for copy in vis_copies:
+        copy.wait()
+    transform(range(tiles // 2))
     pl.semaphore_wait(barrier, n - 1)
 
     def send_comp(offset):
@@ -101,18 +115,7 @@
 
     peers(send_comp)
 
-    for copy in vis_copies:
-        copy.wait()
-    rows = 2 * tiles
-    for tile in range(tiles):
-        parts = [vis[pl.ds(2 * tile + c, ticks, stride=rows), :] for c in range(2)]
-        high, low = split(jnp.concatenate(parts, 1))
-        product = mul(all_rows, high)
-        product = product[: 2 * n] + product[2 * n :] + mul(high_rows, low)
-        real = product[:n, :LANES] + product[n:, LANES:]
-        imag = product[:n, LANES:] - product[n:, :LANES]
-        spec_out[:, tile, :] = real
-        spec_out[:, tiles + tile, :] = imag
+    transform(range(tiles // 2, tiles))
 
     def send_spec(offset):
         pltpu.make_async_remote_copy(

time: 11.1 us -> 11.8 us (1.063)
  Pallas kernels: 9.71 us -> 10.4 us
    pallas_call x1, Pallas kernels: 9.71 us -> 10.4 us  [body(): pl.pallas_call(functools.partial(kernel, n, ticks, tiles, count, width, p...]
where the time goes in v7:
time: 11.8 us; the launch traced here: 11.7 us
  Pallas kernels  10.4 us (88%)
  between operations  0.66 us (6%)
  local copies, waits for them, and re-layouts  0.6 us (5%)
    pallas_call x1, Pallas kernels, body(): pl.pallas_call(functools.partial(kernel, n, ticks, tiles, count, width, p...  10.4 us
    unnamed x1, local copies, waits for them, and re-layouts  0.6 us

profile of v7, /device:TPU:0, one launch (start us, length us, event | category | flops | bytes accessed | tf_op | source)
XLA Modules:
  0.0 11.7 jit_solution(10150442228956812734)
XLA Ops:
  0.7 10.4 %shard_map.55 = f32[16,128]{1,0:T(8,128)S(1)} custom-call(s32[1]{0:T(128)S(6)} %copy.10.start_ref, f32[2048,128]{1,0:T(8,128)} %bitcast.14, bf16[512,1024]{1,0:T(8,128)(2,1)} %bitcast.15, s32[1,64]{1,0:T(1,128)} %bitcast.17, s32[2,64]{1,0:T(2,128)} %bitcast.16), custom_call_target="tpu_custom_call" | custom-call | flops 20971520 | bytes 2097152 | tf_op jit(solution)/shard_map/pallas_call | solution.py:193
  11.1 0.6 %copy.9 = f32[1,2,1024]{2,1,0:T(2,128)} copy(f32[1,2,1024]{2,1,0:T(2,128)S(1)} %bitcast.13) | data formatting | bytes 16384

commit v8 on v7

--- a/solution.py
+++ b/solution.py
@@ -89,7 +89,7 @@
     amp_copy.wait()
     comp_out[0:1, 0:count] = index_ref[...]
     comp_out[1:3, 0:count] = amp_ref[...]
-    comp_in[n - 1] = comp_out[...]
+    comp_in[(n - 1) * 8 : n * 8, :] = comp_out[...]
     def transform(some_tiles):
         for tile in some_tiles:
             parts = [vis[pl.ds(2 * tile + c, ticks, stride=2 * tiles), :] for c in range(2)]
@@ -108,7 +108,7 @@
 
     def send_comp(offset):
         pltpu.make_async_remote_copy(
-            src_ref=comp_out, dst_ref=comp_in.at[offset - 1],
+            src_ref=comp_out, dst_ref=comp_in.at[pl.ds(pl.multiple_of((offset - 1) * 8, 8), 8)],
             send_sem=comp_send, recv_sem=comp_recv,
             device_id={"ma": peer(offset)}, device_id_type=MESH,
         ).start()
@@ -126,9 +126,9 @@
 
     peers(send_spec)
 
-    arrived = comp_in.at[pl.ds(0, n - 1)]
+    arrived = comp_in.at[pl.ds(0, (n - 1) * 8)]
     pltpu.make_async_copy(arrived, arrived, comp_recv).wait()
-    fields = [comp_in[:, row, :] for row in range(3)]
+    fields = [comp_in[pl.ds(row, n, stride=8), :] for row in range(3)]
     if 2 * count == LANES and n % 2 == 0:
         fields = [jnp.concatenate([f[: n // 2, :count], f[n // 2 :, :count]], 1) for f in fields]
     index = fields[0] - me * width
@@ -172,7 +172,7 @@
         out_ref[2 * block : 2 * block + 2, :] = alm[:, block * LANES : (block + 1) * LANES]
 
     for buffer, sem in ((comp_in, comp_send), (spec_in, spec_send)):
-        sent = buffer.at[pl.ds(0, n - 1)]
+        sent = buffer.at[pl.ds(0, buffer.shape[0] // n * (n - 1))]
         pltpu.make_async_copy(sent, sent, sem).wait()
 
 
@@ -203,8 +203,8 @@
             pltpu.VMEM((2 * lines, width), BF16),
             pltpu.VMEM((1, count), jnp.int32),
             pltpu.VMEM((2, count), jnp.int32),
-            pltpu.VMEM((4, LANES), jnp.int32),
-            pltpu.VMEM((n, 4, LANES), jnp.int32),
+            pltpu.VMEM((8, LANES), jnp.int32),
+            pltpu.VMEM((n * 8, LANES), jnp.int32),
             pltpu.VMEM((n, 2 * tiles, LANES), F32),
             pltpu.VMEM((n, 2 * tiles, LANES), F32),
         ]

time: 11.8 us -> 11.9 us (level)
  no operation moved by 1% of the time
where the time goes in v8:
time: 11.9 us; the launch traced here: 11.7 us
  Pallas kernels  10.4 us (87%)
  between operations  0.66 us (6%)
  local copies, waits for them, and re-layouts  0.6 us (5%)
    pallas_call x1, Pallas kernels, body(): pl.pallas_call(functools.partial(kernel, n, ticks, tiles, count, width, p...  10.4 us
    unnamed x1, local copies, waits for them, and re-layouts  0.6 us

profile of v8, /device:TPU:0, one launch (start us, length us, event | category | flops | bytes accessed | tf_op | source)
XLA Modules:
  0.0 11.7 jit_solution(6071770348232965953)
XLA Ops:
  0.7 10.4 %shard_map.55 = f32[16,128]{1,0:T(8,128)S(1)} custom-call(s32[1]{0:T(128)S(6)} %copy.10.start_ref, f32[2048,128]{1,0:T(8,128)} %bitcast.14, bf16[512,1024]{1,0:T(8,128)(2,1)} %bitcast.15, s32[1,64]{1,0:T(1,128)} %bitcast.17, s32[2,64]{1,0:T(2,128)} %bitcast.16), custom_call_target="tpu_custom_call" | custom-call | flops 20971520 | bytes 2097152 | tf_op jit(solution)/shard_map/pallas_call | solution.py:193
  11.1 0.6 %copy.9 = f32[1,2,1024]{2,1,0:T(2,128)} copy(f32[1,2,1024]{2,1,0:T(2,128)S(1)} %bitcast.13) | data formatting | bytes 16384

commit v9 on v6

--- a/solution.py
+++ b/solution.py
@@ -58,8 +58,6 @@
         part = pl.ds(i * piece, piece)
         vis_copies.append(pltpu.make_async_copy(vis_hbm.at[part], vis.at[part], vis_sem.at[i]))
     transfer_copy = pltpu.make_async_copy(transfer_hbm, transfer, transfer_sem)
-    for copy in (index_copy, amp_copy, *vis_copies, transfer_copy):
-        copy.start()
 
     def peers(step):
         if n <= 32:
@@ -78,6 +76,8 @@
         pl.semaphore_signal(barrier, inc=1, device_id={"ma": peer(offset)}, device_id_type=MESH)
 
     peers(greet)
+    for copy in (index_copy, amp_copy, *vis_copies, transfer_copy):
+        copy.start()
 
     cos, sin = trig_pair(start_ref[0], me * ticks, n, ticks, ticks * n)
     (cos_high, cos_low), (sin_high, sin_low) = split(cos), split(sin)

time: 11.1 us -> 11.3 us (1.018)
  Pallas kernels: 9.71 us -> 9.88 us
    pallas_call x1, Pallas kernels: 9.71 us -> 9.88 us  [body(): pl.pallas_call(functools.partial(kernel, n, ticks, tiles, count, width, p...]
where the time goes in v9:
time: 11.3 us; the launch traced here: 11.1 us
  Pallas kernels  9.88 us (87%)
  between operations  0.66 us (6%)
  local copies, waits for them, and re-layouts  0.6 us (5%)
    pallas_call x1, Pallas kernels, body(): pl.pallas_call(functools.partial(kernel, n, ticks, tiles, count, width, p...  9.88 us
    unnamed x1, local copies, waits for them, and re-layouts  0.6 us

profile of v9, /device:TPU:0, one launch (start us, length us, event | category | flops | bytes accessed | tf_op | source)
XLA Modules:
  0.0 11.1 jit_solution(1107002378683193618)
XLA Ops:
  0.7 9.9 %shard_map.55 = f32[16,128]{1,0:T(8,128)S(1)} custom-call(s32[1]{0:T(128)S(6)} %copy.10.start_ref, f32[2048,128]{1,0:T(8,128)} %bitcast.14, bf16[512,1024]{1,0:T(8,128)(2,1)} %bitcast.15, s32[1,64]{1,0:T(1,128)} %bitcast.17, s32[2,64]{1,0:T(2,128)} %bitcast.16), custom_call_target="tpu_custom_call" | custom-call | flops 20971520 | bytes 2097152 | tf_op jit(solution)/shard_map/pallas_call | solution.py:190
  10.5 0.6 %copy.9 = f32[1,2,1024]{2,1,0:T(2,128)} copy(f32[1,2,1024]{2,1,0:T(2,128)S(1)} %bitcast.13) | data formatting | bytes 16384
